TPU v7x, 32 devices: a whole 2x2x4 slice. The times are simulated.
32 devices in a mesh: gr: 8 (over y, x, core), gc: 4 (over z).
Axes of the slice: x: 2, y: 2, z: 4, core: 2. Of those that a mesh axis runs over, the one named last changes fastest.
Arguments:
- features: bfloat16 [4, 8, 512, 128], P('gc', 'gr'), may hold values from -6 to 6
- out_grad: bfloat16 [8, 4, 512, 128], P('gr', 'gc'), may hold values from -6 to 6
- weight: bfloat16 [128, 128], replicated, may hold values from -0.5 to 0.5
- block_values: bfloat16 [8, 4, 128, 128, 128], P('gr', 'gc'), may hold values from 0 to 0.03491211
- block_slot: int32 [8, 4, 128], P('gr', 'gc'), may hold values from 0 to 127, as said below
- live_count: int32 [8, 4], P('gr', 'gc'), may hold values from 32 to 128, as said below
- row_need: int32 [8, 4, 4, 2], P('gr', 'gc'), may hold values from 0 to 3, as said below
- col_need: int32 [8, 4, 8, 2], P('gr', 'gc'), may hold values from 0 to 3, as said below
Outputs:
- activated: bfloat16 [8, 4, 512, 128], P('gr', 'gc')
- weight_grad: float32 [128, 128], replicated
- input_grad: bfloat16 [4, 8, 512, 128], P('gc', 'gr')
Inputs may be any that keep to these rules, and one draw needn't show every extreme that they name: `block_slot`: within one tile the 128 entries are distinct. `live_count`: each tile holds 128, 64 or 32 live slots; some tile holds 128 in every draw. `row_need`: the 2 entries for one tile and one owner are distinct. `col_need`: the 2 entries for one tile and one owner are distinct.
All inputs are finite; a program needn't handle non-finite values.
Results may differ from a plain program's by a relative error of at most 0.0069.
Values may be sent and summed in bfloat16 or wider, within the bound.
A program may use at most 64 MiB of HBM per device.

v0:
```python
import jax
import jax.numpy as jnp
from jax import lax
from jax.sharding import PartitionSpec as P


def add_blocks(arrived, asked, per_dev):
    onehot = (jnp.arange(per_dev)[:, None] == asked[None, :]).astype(jnp.bfloat16)
    return jnp.dot(onehot, arrived, preferred_element_type=jnp.float32)


def on_device(features, out_grad, weight, block_values, block_slot, live_count, row_need, col_need):
    n_rows = lax.axis_size("gr")
    n_cols = lax.axis_size("gc")
    values = block_values[0, 0]
    slot_total = values.shape[0]
    blk = values.shape[1]
    local = features.shape[2]
    width = features.shape[3]
    per_dev = local // blk
    cap = row_need.shape[3]
    col_slots = n_rows * cap
    row_slots = n_cols * cap
    slots = block_slot[0, 0]
    live = jnp.arange(slot_total) < live_count[0, 0]
    row_of = slots // col_slots
    col_of = slots % col_slots
    row_target = jnp.where(live, row_of, row_slots)
    col_target = jnp.where(live, col_of, col_slots)
    row_asked = lax.all_to_all(row_need, "gc", split_axis=2, concat_axis=0, tiled=True).reshape(
        row_slots
    )
    col_asked = lax.all_to_all(col_need, "gr", split_axis=2, concat_axis=0, tiled=True).reshape(
        col_slots
    )
    gathered = lax.all_gather(features, "gr", axis=1, tiled=True).reshape(
        n_rows, per_dev, blk, width
    )
    picked = gathered[jnp.arange(n_rows)[:, None], col_need[0, 0]].reshape(col_slots, blk, width)
    terms = jnp.einsum("bmk,bkf->bmf", values, picked[col_of], preferred_element_type=jnp.float32)
    partial_value = jax.ops.segment_sum(terms, row_target, num_segments=row_slots + 1)[
        :row_slots
    ].astype(jnp.bfloat16)
    arrived = lax.all_to_all(
        partial_value.reshape(n_cols, cap, blk, width),
        "gc",
        split_axis=0,
        concat_axis=0,
        tiled=True,
    )
    aggregated = add_blocks(arrived.reshape(row_slots, blk * width), row_asked, per_dev)
    aggregated = aggregated.astype(jnp.bfloat16).reshape(local, width)
    pre = jnp.dot(aggregated, weight, preferred_element_type=jnp.float32)
    sig = jax.nn.sigmoid(pre)
    activated = (pre * sig).astype(jnp.bfloat16)
    upstream = out_grad[0, 0].astype(jnp.float32)
    grad_pre = (upstream * sig * (1.0 + pre * (1.0 - sig))).astype(jnp.bfloat16)
    local_term = lax.dot_general(
        aggregated, grad_pre, (((0,), (0,)), ((), ())), preferred_element_type=jnp.float32
    )
    node_total = local * n_rows * n_cols
    weight_grad = lax.psum(local_term, ("gr", "gc")) * float(node_total) ** (-0.5)
    back_rows = lax.dot_general(
        grad_pre, weight, (((1,), (1,)), ((), ())), preferred_element_type=jnp.float32
    )
    back_rows = back_rows.astype(jnp.bfloat16)
    outgoing_rows = back_rows.reshape(per_dev, blk, width)[row_asked].reshape(
        n_cols, cap, blk, width
    )
    picked_rows = lax.all_to_all(
        outgoing_rows, "gc", split_axis=0, concat_axis=0, tiled=True
    ).reshape(row_slots, blk, width)
    back_terms = jnp.einsum(
        "bmk,bmf->bkf", values, picked_rows[row_of], preferred_element_type=jnp.float32
    )
    partial_back = jax.ops.segment_sum(back_terms, col_target, num_segments=col_slots + 1)[
        :col_slots
    ].astype(jnp.bfloat16)
    returned = lax.all_to_all(
        partial_back.reshape(n_rows, cap, blk, width), "gr", split_axis=0, concat_axis=0, tiled=True
    )
    input_grad = add_blocks(returned.reshape(col_slots, blk * width), col_asked, per_dev)
    input_grad = input_grad.astype(jnp.bfloat16).reshape(1, 1, local, width)
    return (activated.reshape(1, 1, local, width), weight_grad, input_grad)


def solution(mesh):
    placed = (
        P("gc", "gr", None, None),
        P("gr", "gc", None, None),
        P(),
        P("gr", "gc", None, None, None),
        P("gr", "gc", None),
        P("gr", "gc"),
        P("gr", "gc", None, None),
        P("gr", "gc", None, None),
    )
    return jax.shard_map(
        on_device,
        mesh=mesh,
        in_specs=placed,
        out_specs=(P("gr", "gc", None, None), P(), P("gc", "gr", None, None)),
        check_vma=False,
    )
```

profile of v0, /device:TPU:25, one launch (start us, length us, event | category | flops | bytes accessed | tf_op | source)
XLA Modules:
  0.0 283.6 jit_solution(8673407214740214383)
XLA Ops:
  7.2 0.0 copy-start
  7.2 0.0 all-gather.2.cloned.1.call-start
  7.2 0.7 all-gather.2.cloned.1.call-update
  7.9 1.3 copy.25
  9.3 4.5 %all-to-all-start = ((s32[1,1,4,2]{3,1,0,2:T(1,128)}), s32[1,1,4,2]{3,1,0,2:T(1,128)S(1)}, u32[]{:S(2)}, u32[]{:S(2)}) async-start(s32[1,1,4,2]{3,1,0,2:T(1,128)} %copy.25), calls=%async_computation | async-start | bytes 4096 | tf_op jit(solution)/shard_map/all_to_all | solution.py:30
  14.4 0.7 fusion.19
  15.1 0.1 copy.27
  15.2 0.1 reshape.288
  15.3 0.7 fusion.26
  16.0 18.9 %all-gather.2.cloned.1.call-done = bf16[1,8,512,128]{3,2,0,1:T(8,128)(2,1)} async-done(((bf16[1,1,512,128]{3,2,0,1:T(8,128)(2,1)}), bf16[1,8,512,128]{3,2,0,1:T(8,128)(2,1)}) %all-gather.2.cloned.1.call-update) | async-done | bytes 1048592 | tf_op jit(solution)/shard_map/all_gather | solution.py:36
  34.8 1.9 gather_fusion
  36.7 3.0 %gather_fusion.1 = bf16[128,128,128]{2,1,0:T(8,128)(2,1)} fusion(bf16[16,128,128]{2,1,0:T(8,128)(2,1)S(1)} %gather_fusion, s32[1024]{0:T(1024)S(1)} %pad_clamp_fusion.2), kind=kCustom, calls=%fused_computation.1 | custom fusion | bytes 8389120 | tf_op jit(solution)/shard_map/gather | solution.py:40
  39.8 9.8 %fusion.4 = f32[128,128,128]{1,2,0:T(8,128)} fusion(bf16[128,128,128]{2,1,0:T(8,128)(2,1)} %gather_fusion.1, bf16[1,1,128,128,128]{4,3,2,1,0:T(8,128)(2,1)} %param.11), kind=kOutput, calls=%fused_computation.12 | convolution fusion | flops 536870912 | bytes 16777216 | tf_op jit(solution)/shard_map/bmk,bkf->bmf/dot_general | solution.py:40
  49.5 9.0 %copy.29 = f32[128,128,128]{2,1,0:T(8,128)} copy(f32[128,128,128]{1,2,0:T(8,128)} %fusion.4) | data formatting | bytes 16777216 | tf_op jit(solution)/shard_map/bmk,bkf->bmf/dot_general | solution.py:40
  58.6 0.0 copy-start.2
  58.6 17.0 %scatter_fusion = f32[9,128,128]{2,1,0:T(8,128)S(1)} fusion(f32[9,128,128]{2,1,0:T(8,128)S(1)} %broadcast_in_dim.11, s32[128]{0:T(128)S(1)} %get-tuple-element.10, f32[128,128,128]{2,1,0:T(8,128)} %copy.29), kind=kCustom, calls=%fused_computation.4 | custom fusion | flops 2097152 | bytes 25166336 | tf_op jit(solution)/shard_map/scatter-add | solution.py:41
  75.6 0.0 copy-start.1
  75.6 0.7 slice.23
  76.4 0.0 all-to-all-done
  76.4 4.5 %all-to-all-start.1 = ((bf16[4,2,128,128]{3,2,1,0:T(8,128)(2,1)}), bf16[4,2,128,128]{3,2,1,0:T(8,128)(2,1)S(1)}, u32[]{:S(2)}, u32[]{:S(2)}) async-start(bf16[4,2,128,128]{3,2,1,0:T(8,128)(2,1)} %bitcast.9), calls=%async_computation.1 | async-start | bytes 524288 | tf_op jit(solution)/shard_map/all_to_all | solution.py:44
  80.9 0.5 broadcast.290
  81.4 0.7 reduce.8
  82.1 0.1 eq.33
  82.2 0.1 reshape.281
  82.3 5.0 %all-to-all-done.1 = bf16[4,2,128,128]{3,2,1,0:T(8,128)(2,1)S(1)} async-done(((bf16[4,2,128,128]{3,2,1,0:T(8,128)(2,1)}), bf16[4,2,128,128]{3,2,1,0:T(8,128)(2,1)S(1)}, u32[]{:S(2)}, u32[]{:S(2)}) %all-to-all-start.1) | async-done | bytes 262176 | tf_op jit(solution)/shard_map/all_to_all | solution.py:44
  87.2 0.3 convolution_convert_fusion.1
  87.5 0.2 reshape.278
  87.7 0.0 copy-done
  87.7 0.0 copy-done.2
  87.7 0.9 fusion.15
  88.6 0.2 convolution_convert_fusion.2
  88.8 1.3 gather_fusion.2
  90.1 4.5 %all-to-all-start.3 = ((bf16[4,2,128,128]{3,2,1,0:T(8,128)(2,1)}), bf16[4,2,128,128]{3,2,1,0:T(8,128)(2,1)S(1)}, u32[]{:S(2)}, u32[]{:S(2)}) async-start(bf16[4,2,128,128]{3,2,1,0:T(8,128)(2,1)} %bitcast.15), calls=%async_computation.3 | async-start | bytes 524288 | tf_op jit(solution)/shard_map/all_to_all | solution.py:70
  94.6 0.0 copy-done.1
  94.6 0.7 copy.30
  95.3 3.6 %all-to-all-done.3 = bf16[4,2,128,128]{3,2,1,0:T(8,128)(2,1)S(1)} async-done(((bf16[4,2,128,128]{3,2,1,0:T(8,128)(2,1)}), bf16[4,2,128,128]{3,2,1,0:T(8,128)(2,1)S(1)}, u32[]{:S(2)}, u32[]{:S(2)}) %all-to-all-start.3) | async-done | bytes 262176 | tf_op jit(solution)/shard_map/all_to_all | solution.py:70
  98.9 6.7 %all-to-all-start.2 = ((s32[1,1,8,2]{3,1,0,2:T(1,128)}), s32[1,1,8,2]{3,1,0,2:T(1,128)S(1)}, u32[]{:S(2)}, u32[]{:S(2)}) async-start(s32[1,1,8,2]{3,1,0,2:T(1,128)} %copy.30), calls=%async_computation.2 | async-start | bytes 8192 | tf_op jit(solution)/shard_map/all_to_all | solution.py:33
  105.6 3.0 %gather_fusion.3 = bf16[128,128,128]{2,1,0:T(8,128)(2,1)} fusion(bf16[8,128,128]{2,1,0:T(8,128)(2,1)S(1)} %bitcast.75, s32[1024]{0:T(1024)S(1)} %pad_clamp_fusion), kind=kCustom, calls=%fused_computation.3 | custom fusion | bytes 8389120 | tf_op jit(solution)/shard_map/gather | solution.py:74
  108.6 8.2 %fusion.7 = f32[128,128,128]{1,2,0:T(8,128)} fusion(bf16[128,128,128]{2,1,0:T(8,128)(2,1)} %gather_fusion.3, bf16[1,1,128,128,128]{4,3,2,1,0:T(8,128)(2,1)} %param.11), kind=kOutput, calls=%fused_computation.13 | convolution fusion | flops 536870912 | bytes 16777216 | tf_op jit(solution)/shard_map/bmk,bmf->bkf/dot_general | solution.py:73
  116.9 9.0 %copy.32 = f32[128,128,128]{2,1,0:T(8,128)} copy(f32[128,128,128]{1,2,0:T(8,128)} %fusion.7) | data formatting | bytes 16777216 | tf_op jit(solution)/shard_map/bmk,bmf->bkf/dot_general | solution.py:73
  125.8 0.1 broadcast_in_dim.14
  126.0 17.0 %scatter_fusion.1 = f32[17,128,128]{2,1,0:T(8,128)S(1)} fusion(f32[17,128,128]{2,1,0:T(8,128)S(1)} %broadcast_in_dim.14, s32[128]{0:T(128)S(1)} %get-tuple-element.8, f32[128,128,128]{2,1,0:T(8,128)} %copy.32), kind=kCustom, calls=%fused_computation.5 | custom fusion | flops 2097152 | bytes 25166336 | tf_op jit(solution)/shard_map/scatter-add | solution.py:76
  143.0 0.9 slice.22
  143.9 0.0 all-to-all-done.2
  143.9 4.2 %all-to-all-start.4 = ((bf16[8,2,128,128]{3,2,1,0:T(8,128)(2,1)}), bf16[8,2,128,128]{3,2,1,0:T(8,128)(2,1)S(1)}, u32[]{:S(2)}, u32[]{:S(2)}) async-start(bf16[8,2,128,128]{3,2,1,0:T(8,128)(2,1)} %bitcast.19), calls=%async_computation.4 | async-start | bytes 1048576 | tf_op jit(solution)/shard_map/all_to_all | solution.py:79
  148.1 0.0 all-reduce.2.cloned.1.call-start
  148.1 0.9 fusion.27
  149.0 0.0 all-reduce.2.cloned.1.call-update
  149.0 0.7 reduce.9
  149.7 0.1 eq.37
  149.7 124.4 %all-reduce.2.cloned.1.call-done = f32[128,128]{1,0:T(8,128)} async-done(((f32[128,128]{1,0:T(8,128)}), f32[128,128]{1,0:T(8,128)}) %all-reduce.2.cloned.1.call-update) | async-done | bytes 65552 | tf_op jit(solution)/shard_map/psum | solution.py:62
  274.1 1.5 broadcast_multiply_fusion
  275.6 0.0 all-to-all-done.4
  275.6 0.4 convolution_convert_fusion
  276.0 0.8 reshape.286
  (6 shorter events, 0.1 us)
Async XLA Ops:
  7.2 80.5 %copy-start = (bf16[128,128]{1,0:T(8,128)(2,1)S(1)}, bf16[128,128]{1,0:T(8,128)(2,1)}, u32[]{:S(2)}) copy-start(bf16[128,128]{1,0:T(8,128)(2,1)} %param.10) | copy-start | bytes 98308
  7.2 27.7 %all-gather.2.cloned.1.call-start = ((), (), s32[]{:S(2)}) async-start(), calls=%async_computation.5 | async-start | bytes 1179648 | tf_op jit(solution)/shard_map/all_gather | solution.py:36
  9.3 67.1 %all-to-all-start = ((s32[1,1,4,2]{3,1,0,2:T(1,128)}), s32[1,1,4,2]{3,1,0,2:T(1,128)S(1)}, u32[]{:S(2)}, u32[]{:S(2)}) async-start(s32[1,1,4,2]{3,1,0,2:T(1,128)} %copy.25), calls=%async_computation | async-start | bytes 4096 | tf_op jit(solution)/shard_map/all_to_all | solution.py:30
  58.6 29.1 %copy-start.2 = (bf16[1,1,512,128]{3,2,1,0:T(8,128)(2,1)S(1)}, bf16[1,1,512,128]{3,2,1,0:T(8,128)(2,1)}, u32[]{:S(2)}) copy-start(bf16[1,1,512,128]{3,2,1,0:T(8,128)(2,1)} %param.9) | copy-start | bytes 393220
  75.6 19.0 %copy-start.1 = (s32[1,1,8,2]{2,3,1,0:T(2,128)S(1)}, s32[1,1,8,2]{2,3,1,0:T(2,128)}, u32[]{:S(2)}) copy-start(s32[1,1,8,2]{2,3,1,0:T(2,128)} %param.15) | copy-start | bytes 196
  76.4 10.9 %all-to-all-start.1 = ((bf16[4,2,128,128]{3,2,1,0:T(8,128)(2,1)}), bf16[4,2,128,128]{3,2,1,0:T(8,128)(2,1)S(1)}, u32[]{:S(2)}, u32[]{:S(2)}) async-start(bf16[4,2,128,128]{3,2,1,0:T(8,128)(2,1)} %bitcast.9), calls=%async_computation.1 | async-start | bytes 524288 | tf_op jit(solution)/shard_map/all_to_all | solution.py:44
  90.1 8.8 %all-to-all-start.3 = ((bf16[4,2,128,128]{3,2,1,0:T(8,128)(2,1)}), bf16[4,2,128,128]{3,2,1,0:T(8,128)(2,1)S(1)}, u32[]{:S(2)}, u32[]{:S(2)}) async-start(bf16[4,2,128,128]{3,2,1,0:T(8,128)(2,1)} %bitcast.15), calls=%async_computation.3 | async-start | bytes 524288 | tf_op jit(solution)/shard_map/all_to_all | solution.py:70
  98.9 45.0 %all-to-all-start.2 = ((s32[1,1,8,2]{3,1,0,2:T(1,128)}), s32[1,1,8,2]{3,1,0,2:T(1,128)S(1)}, u32[]{:S(2)}, u32[]{:S(2)}) async-start(s32[1,1,8,2]{3,1,0,2:T(1,128)} %copy.30), calls=%async_computation.2 | async-start | bytes 8192 | tf_op jit(solution)/shard_map/all_to_all | solution.py:33
  143.9 131.7 %all-to-all-start.4 = ((bf16[8,2,128,128]{3,2,1,0:T(8,128)(2,1)}), bf16[8,2,128,128]{3,2,1,0:T(8,128)(2,1)S(1)}, u32[]{:S(2)}, u32[]{:S(2)}) async-start(bf16[8,2,128,128]{3,2,1,0:T(8,128)(2,1)} %bitcast.19), calls=%async_computation.4 | async-start | bytes 1048576 | tf_op jit(solution)/shard_map/all_to_all | solution.py:79
  148.1 126.0 %all-reduce.2.cloned.1.call-start = ((), (), s32[]{:S(2)}) async-start(), calls=%async_computation.6 | async-start | bytes 131072 | tf_op jit(solution)/shard_map/psum | solution.py:62
Sparse Core Ops, SparseCore 0:
  9.9 24.8 all-gather.1
  155.1 118.9 all-reduce.1
where the time goes:
time: 287 us; the launch traced here: 284 us
  waiting for transfers between devices  152 us (53%)
  other arithmetic  38.3 us (13%)
  local copies, waits for them, and re-layouts  32.9 us (11%)
  starting transfers between devices  24.6 us (9%)
  matrix products  20.6 us (7%)
  between operations  14.8 us (5%)
    psum x1, waiting for transfers between devices, on_device(): lax.psum(local_term, ('gr', 'gc')) * float(node_total) ** (-0.5)  124 us
    all_gather x1, waiting for transfers between devices, on_device(): lax.all_gather(features, 'gr', axis=1, tiled=True)  18.9 us
    scatter-add x1, other arithmetic, on_device(): jax.ops.segment_sum(back_terms, col_target, num_segments=col_slots + 1)  17 us
    scatter-add x1, other arithmetic, on_device(): jax.ops.segment_sum(terms, row_target, num_segments=row_slots + 1)  17 us
    dot_general x1, matrix products, on_device(): jnp.einsum('bmk,bkf->bmf', values, picked[col_of], preferred_element_type...  9.78 us
    dot_general x1, local copies, waits for them, and re-layouts, on_device(): jnp.einsum('bmk,bkf->bmf', values, picked[col_of], preferred_element_type...  8.97 us
    dot_general x1, local copies, waits for them, and re-layouts, on_device(): jnp.einsum('bmk,bmf->bkf', values, picked_rows[row_of], preferred_element...  8.97 us
    dot_general x1, matrix products, on_device(): jnp.einsum('bmk,bmf->bkf', values, picked_rows[row_of], preferred_element...  8.24 us
  transfers between devices with their start and end apart: 7, of which 4 were waited for; matrix products, arithmetic and copies ran while one was open for 31% of the time, Pallas kernels for 0%

commit v1 on v0

v1 whole, which is shorter than its diff:
```python
import functools

import jax
import jax.numpy as jnp
from jax import lax
from jax.experimental import pallas as pl
from jax.experimental.pallas import tpu as pltpu
from jax.sharding import PartitionSpec as P

MESH = pl.DeviceIdType.MESH


def kernel(
    n_rows,
    n_cols,
    cap,
    scale,
    inv,
    col_need,
    row_meta,
    col_meta,
    features,
    out_grad,
    weight,
    values,
    activated,
    weight_grad,
    input_grad,
    vals,
    gathered,
    picked,
    part_out,
    part_in,
    agg,
    back,
    back_out,
    back_in,
    dx_out,
    dx_in,
    row_vm,
    col_vm,
    row_sm,
    col_sm,
    wg_out,
    wg_in,
    wg_piece,
    wg_part,
    wg_done,
    local_sem,
    row_meta_s,
    row_meta_r,
    col_meta_s,
    col_meta_r,
    feat_s,
    feat_r,
    part_s,
    part_r,
    back_s,
    back_r,
    dx_s,
    dx_r,
    wg1_s,
    wg1_r,
    wg2_s,
    wg2_r,
    wg3_s,
    wg3_r,
):
    r_me, c_me = lax.axis_index("gr"), lax.axis_index("gc")
    nzb, blk, _ = values.shape
    per_dev, _, width = features.shape
    col_slots, row_slots = n_rows * cap, n_cols * cap

    def row_at(d):
        return lax.rem(r_me + d, n_rows)

    def col_at(d):
        return lax.rem(c_me + d, n_cols)

    def to_row(d, src, dst, send, recv):
        return pltpu.make_async_remote_copy(
            src_ref=src,
            dst_ref=dst,
            send_sem=send.at[d],
            recv_sem=recv.at[d],
            device_id={"gr": row_at(d)},
            device_id_type=MESH,
        )

    def to_col(d, src, dst, send, recv):
        return pltpu.make_async_remote_copy(
            src_ref=src,
            dst_ref=dst,
            send_sem=send.at[d],
            recv_sem=recv.at[d],
            device_id={"gc": col_at(d)},
            device_id_type=MESH,
        )

    def each(n, body):
        def step(d, carry):
            body(d)
            return carry

        lax.fori_loop(1, n, step, 0)

    load_vals = pltpu.make_async_copy(values, vals.at[pl.ds(0, nzb)], local_sem.at[0])
    load_vals.start()
    mine = pl.ds(r_me * per_dev, per_dev)
    load_own = pltpu.make_async_copy(features, gathered.at[mine], local_sem.at[1])
    load_own.start()

    barrier = pltpu.get_barrier_semaphore()

    def greet_row(d):
        pl.semaphore_signal(barrier, inc=1, device_id={"gr": row_at(d)}, device_id_type=MESH)

    def greet_col(d):
        pl.semaphore_signal(barrier, inc=1, device_id={"gc": col_at(d)}, device_id_type=MESH)

    each(n_rows, greet_row)
    each(n_cols, greet_col)
    pl.semaphore_wait(barrier, n_rows + n_cols - 2)

    def feat_copy(d):
        return to_row(d, features, gathered.at[mine], feat_s, feat_r)

    def row_meta_copy(d):
        return to_col(d, row_meta, row_vm.at[c_me], row_meta_s, row_meta_r)

    def col_meta_copy(d):
        return to_row(d, col_meta, col_vm.at[r_me], col_meta_s, col_meta_r)

    each(n_cols, lambda d: row_meta_copy(d).start())
    each(n_rows, lambda d: col_meta_copy(d).start())
    each(n_rows, lambda d: feat_copy(d).start())

    zero = jnp.zeros((blk, width), jnp.bfloat16)
    vals[nzb] = jnp.zeros((blk, blk), jnp.bfloat16)
    part_in[row_slots] = zero
    dx_in[col_slots] = zero
    row_vm[c_me] = row_meta[...]
    col_vm[r_me] = col_meta[...]

    each(n_cols, lambda d: row_meta_copy(d).wait())
    each(n_rows, lambda d: col_meta_copy(d).wait())
    row_load = pltpu.make_async_copy(row_vm, row_sm, local_sem.at[2])
    col_load = pltpu.make_async_copy(col_vm, col_sm, local_sem.at[3])
    row_load.start()
    col_load.start()
    load_own.wait()
    load_vals.wait()
    each(n_rows, lambda d: feat_copy(d).wait())
    row_load.wait()
    col_load.wait()

    for s in range(col_slots):
        picked[pl.ds(s * blk, blk), :] = gathered[s // cap * per_dev + col_need[s // cap, s % cap]]

    def forward(t):
        left = jnp.concatenate([vals[inv[t * col_slots + s]] for s in range(col_slots)], axis=1)
        total = jnp.dot(left, picked[...], preferred_element_type=jnp.float32)
        return total.astype(jnp.bfloat16)

    def part_copy(d):
        c = col_at(d)
        return to_col(
            d,
            part_out.at[pl.ds(c * cap, cap)],
            part_in.at[pl.ds(c_me * cap, cap)],
            part_s,
            part_r,
        )

    def forward_to(d):
        for k in range(cap):
            part_out[col_at(d) * cap + k] = forward(col_at(d) * cap + k)
        part_copy(d).start()

    each(n_cols, forward_to)
    for k in range(cap):
        part_in[c_me * cap + k] = forward(c_me * cap + k)
    each(n_cols, lambda d: part_copy(d).wait())

    def total_of(ref, asked, n, k):
        total = jnp.zeros((blk, width), jnp.float32)
        for o in range(n):
            place = n * cap
            for q in range(cap):
                place = jnp.where(asked[o][q] == k, o * cap + q, place)
            total = total + ref[place].astype(jnp.float32)
        return total.astype(jnp.bfloat16)

    row_asked = [[row_sm[o, 0, c_me * cap + q] for q in range(cap)] for o in range(n_cols)]
    for k in range(per_dev):
        agg[pl.ds(k * blk, blk), :] = total_of(part_in, row_asked, n_cols, k)
    held = agg[...]
    pre = jnp.dot(held, weight[...], preferred_element_type=jnp.float32)
    sig = jax.nn.sigmoid(pre)
    activated[...] = (pre * sig).astype(jnp.bfloat16)
    upstream = out_grad[...].astype(jnp.float32)
    grad_pre = (upstream * sig * (1.0 + pre * (1.0 - sig))).astype(jnp.bfloat16)
    rows = lax.dot_general(
        grad_pre, weight[...], (((1,), (1,)), ((), ())), preferred_element_type=jnp.float32
    ).astype(jnp.bfloat16)
    for k in range(per_dev):
        back[k] = rows[k * blk : (k + 1) * blk]

    def back_copy(d):
        c = col_at(d)
        return to_col(
            d,
            back_out.at[pl.ds(c * cap, cap)],
            back_in.at[pl.ds(c_me * cap, cap)],
            back_s,
            back_r,
        )

    def back_to(d):
        c = col_at(d)
        for k in range(cap):
            back_out[c * cap + k] = back[row_sm[c, 0, c_me * cap + k]]
        back_copy(d).start()

    each(n_cols, back_to)
    for k in range(cap):
        back_in[c_me * cap + k] = back[row_sm[c_me, 0, c_me * cap + k]]

    term = lax.dot_general(
        held, grad_pre, (((0,), (0,)), ((), ())), preferred_element_type=jnp.float32
    )
    piece = term.shape[0] // n_rows
    for o in range(n_rows):
        wg_out[o] = term[o * piece : (o + 1) * piece]
    wg_in[r_me] = wg_out[r_me]

    def wg1_copy(d):
        return to_row(d, wg_out.at[row_at(d)], wg_in.at[r_me], wg1_s, wg1_r)

    def wg2_copy(d):
        return to_col(d, wg_piece, wg_part.at[c_me], wg2_s, wg2_r)

    def wg3_copy(d):
        return to_row(d, wg_piece3, wg_done.at[r_me], wg3_s, wg3_r)

    wg_piece3 = wg_out.at[0]

    each(n_rows, lambda d: wg1_copy(d).start())
    each(n_cols, lambda d: back_copy(d).wait())
    each(n_rows, lambda d: wg1_copy(d).wait())
    total = wg_in[0]
    for o in range(1, n_rows):
        total = total + wg_in[o]
    wg_piece[...] = total
    wg_part[c_me] = total
    each(n_cols, lambda d: wg2_copy(d).start())

    turned = back_in[...].reshape(row_slots * blk, width).T

    def backward(s):
        right = jnp.concatenate(
            [vals[inv[t * col_slots + s]] for t in range(row_slots)], axis=0
        )
        total = jnp.dot(turned, right, preferred_element_type=jnp.float32)
        return total.T.astype(jnp.bfloat16)

    def dx_copy(d):
        r = row_at(d)
        return to_row(
            d,
            dx_out.at[pl.ds(r * cap, cap)],
            dx_in.at[pl.ds(r_me * cap, cap)],
            dx_s,
            dx_r,
        )

    def backward_to(d):
        for k in range(cap):
            dx_out[row_at(d) * cap + k] = backward(row_at(d) * cap + k)
        dx_copy(d).start()

    each(n_rows, backward_to)
    for k in range(cap):
        dx_in[r_me * cap + k] = backward(r_me * cap + k)

    each(n_cols, lambda d: wg2_copy(d).wait())
    total = wg_part[0]
    for o in range(1, n_cols):
        total = total + wg_part[o]
    total = total * scale
    wg_out[0] = total
    wg_done[r_me] = total
    each(n_rows, lambda d: wg3_copy(d).start())

    each(n_rows, lambda d: dx_copy(d).wait())
    col_asked = [[col_sm[o, 0, r_me * cap + q] for q in range(cap)] for o in range(n_rows)]
    for k in range(per_dev):
        input_grad[pl.ds(k * blk, blk), :] = total_of(dx_in, col_asked, n_rows, k)
    each(n_rows, lambda d: wg3_copy(d).wait())
    for o in range(n_rows):
        weight_grad[pl.ds(o * piece, piece), :] = wg_done[o]


def on_device(features, out_grad, weight, block_values, block_slot, live_count, row_need, col_need):
    n_rows = lax.axis_size("gr")
    n_cols = lax.axis_size("gc")
    values = block_values[0, 0]
    nzb, blk, _ = values.shape
    local, width = features.shape[2:]
    per_dev = local // blk
    cap = row_need.shape[3]
    col_slots = n_rows * cap
    row_slots = n_cols * cap
    place = jnp.arange(col_slots * row_slots)
    block = jnp.arange(nzb)
    match = (block_slot[0, 0][None, :] == place[:, None]) & (block < live_count[0, 0])[None, :]
    inv = jnp.min(jnp.where(match, block[None, :], nzb), axis=1).astype(jnp.int32)

    def padded(need):
        flat = need.reshape(1, -1)
        return jnp.pad(flat, ((0, 0), (0, -flat.shape[1] % 128)))

    row_meta = padded(row_need)
    col_meta = padded(col_need)
    bf, f32, i32 = jnp.bfloat16, jnp.float32, jnp.int32
    piece = width // n_rows
    dma = pltpu.SemaphoreType.DMA
    vmem = pl.BlockSpec(memory_space=pltpu.VMEM)
    smem = pl.BlockSpec(memory_space=pltpu.SMEM)
    hbm = pl.BlockSpec(memory_space=pl.ANY)
    scale = float(local * n_rows * n_cols) ** (-0.5)
    flops = 4 * nzb * blk * blk * width
    activated, weight_grad, input_grad = pl.pallas_call(
        functools.partial(kernel, n_rows, n_cols, cap, scale),
        out_shape=(
            jax.ShapeDtypeStruct((local, width), bf),
            jax.ShapeDtypeStruct((width, width), f32),
            jax.ShapeDtypeStruct((local, width), bf),
        ),
        in_specs=[smem, smem, vmem, vmem, hbm, vmem, vmem, hbm],
        out_specs=(vmem, vmem, vmem),
        scratch_shapes=[
            pltpu.VMEM((nzb + 1, blk, blk), bf),
            pltpu.VMEM((n_rows * per_dev, blk, width), bf),
            pltpu.VMEM((col_slots * blk, width), bf),
            pltpu.VMEM((row_slots, blk, width), bf),
            pltpu.VMEM((row_slots + 1, blk, width), bf),
            pltpu.VMEM((local, width), bf),
            pltpu.VMEM((per_dev, blk, width), bf),
            pltpu.VMEM((row_slots, blk, width), bf),
            pltpu.VMEM((row_slots, blk, width), bf),
            pltpu.VMEM((col_slots, blk, width), bf),
            pltpu.VMEM((col_slots + 1, blk, width), bf),
            pltpu.VMEM((n_cols,) + row_meta.shape, i32),
            pltpu.VMEM((n_rows,) + col_meta.shape, i32),
            pltpu.SMEM((n_cols,) + row_meta.shape, i32),
            pltpu.SMEM((n_rows,) + col_meta.shape, i32),
            pltpu.VMEM((n_rows, piece, width), f32),
            pltpu.VMEM((n_rows, piece, width), f32),
            pltpu.VMEM((piece, width), f32),
            pltpu.VMEM((n_cols, piece, width), f32),
            pltpu.VMEM((n_rows, piece, width), f32),
            dma((4,)),
            dma((n_cols,)),
            dma((n_cols,)),
            dma((n_rows,)),
            dma((n_rows,)),
            dma((n_rows,)),
            dma((n_rows,)),
            dma((n_cols,)),
            dma((n_cols,)),
            dma((n_cols,)),
            dma((n_cols,)),
            dma((n_rows,)),
            dma((n_rows,)),
            dma((n_rows,)),
            dma((n_rows,)),
            dma((n_cols,)),
            dma((n_cols,)),
            dma((n_rows,)),
            dma((n_rows,)),
        ],
        compiler_params=pltpu.CompilerParams(
            collective_id=0, has_side_effects=True, vmem_limit_bytes=48 * 2**20
        ),
        cost_estimate=pl.CostEstimate(
            flops=flops, bytes_accessed=values.size * 2, transcendentals=0
        ),
    )(
        inv,
        col_need[0, 0],
        row_meta,
        col_meta,
        features.reshape(per_dev, blk, width),
        out_grad.reshape(local, width),
        weight,
        values,
    )
    shape = (1, 1, local, width)
    return activated.reshape(shape), weight_grad, input_grad.reshape(shape)


def solution(mesh):
    placed = (
        P("gc", "gr", None, None),
        P("gr", "gc", None, None),
        P(),
        P("gr", "gc", None, None, None),
        P("gr", "gc", None),
        P("gr", "gc"),
        P("gr", "gc", None, None),
        P("gr", "gc", None, None),
    )
    return jax.shard_map(
        on_device,
        mesh=mesh,
        in_specs=placed,
        out_specs=(P("gr", "gc", None, None), P(), P("gc", "gr", None, None)),
        check_vma=False,
    )
```

time: 287 us -> 54.1 us (0.19)
  waiting for transfers between devices: 152 us -> 0 us
  Pallas kernels: 0 us -> 41.8 us
  other arithmetic: 38.3 us -> 0.77 us
  starting transfers between devices: 24.6 us -> 0 us
  local copies, waits for them, and re-layouts: 32.9 us -> 9.15 us
  matrix products: 20.6 us -> 0 us
  between operations: 14.8 us -> 1.31 us
    psum x1 -> x0, waiting for transfers between devices: 124 us -> none  [on_device(): lax.psum(local_term, ('gr', 'gc')) * float(node_total) ** (-0.5)]
    pallas_call x0 -> x1, Pallas kernels: none -> 41.8 us  [on_device(): pl.pallas_call(functools.partial(kernel, n_rows, n_cols, cap, scale), out...]
    scatter-add x2 -> x0, other arithmetic: 34.1 us -> none  [the longest x1 17 us: on_device(): jax.ops.segment_sum(back_terms, col_target, num_segments=col_slots + 1)]
    all_to_all x5 -> x0, starting transfers between devices: 24.5 us -> none  [the longest x1 6.71 us: on_device(): lax.all_to_all(col_need, 'gr', split_axis=2, concat_axis=0, tiled=True)]
    dot_general x7 -> x0, matrix products: 20.6 us -> none  [the longest x1 9.78 us: on_device(): jnp.einsum('bmk,bkf->bmf', values, picked[col_of], preferred_element_type...]
    all_gather x1 -> x0, waiting for transfers between devices: 18.9 us -> none  [on_device(): lax.all_gather(features, 'gr', axis=1, tiled=True)]
    dot_general x2 -> x0, local copies, waits for them, and re-layouts: 17.9 us -> none  [the longest x1 8.97 us: on_device(): jnp.einsum('bmk,bkf->bmf', values, picked[col_of], preferred_element_type...]
    gather x4 -> x0, local copies, waits for them, and re-layouts: 9.24 us -> none  [the longest x1 3.05 us: on_device(): picked[col_of]]
  transfers between devices with their start and end apart: 7 -> 0, of which waited for: 4 -> 0; matrix products, arithmetic and copies ran while one was open for 31% -> 0% of each run, Pallas kernels for 0% -> 0%
where the time goes in v1:
time: 54.1 us; the launch traced here: 53.1 us
  Pallas kernels  41.8 us (77%)
  local copies, waits for them, and re-layouts  9.15 us (17%)
  between operations  1.31 us (2%)
  other arithmetic  0.77 us (1%)
    pallas_call x1, Pallas kernels, on_device(): pl.pallas_call(functools.partial(kernel, n_rows, n_cols, cap, scale), out...  41.8 us
    unnamed x13, local copies, waits for them, and re-layouts  8.21 us

profile of v1, /device:TPU:25, one launch (start us, length us, event | category | flops | bytes accessed | tf_op | source)
XLA Modules:
  0.0 53.1 jit_solution(4483848406799563196)
XLA Ops:
  1.3 0.8 %select_reduce_fusion.inv = s32[128]{0:T(128)S(1)} fusion(s32[128]{0:T(128)} %bitcast.17, pred[128]{0:T(512)(128)(4,1)S(1)} %iota_compare_fusion.1), kind=kLoop, calls=%fused_computation | loop fusion | flops 65408 | bytes 1152 | tf_op jit(solution)/shard_map/reduce_min | solution.py:317
  2.1 0.8 %copy.17 = s32[1,1,4,2]{3,2,1,0:T(4,128)S(1)} copy(s32[1,1,4,2]{2,3,1,0:T(2,128)} %param.14) | data formatting | bytes 64 | tf_op args[6]
  2.8 0.1 reshape.29
  2.9 0.8 %copy.19.col_need = s32[8,2]{1,0:T(8,128)S(1)} copy(s32[8,2]{0,1:T(2,128)} %bitcast.16) | data formatting | bytes 128 | tf_op jit(solution)/shard_map/squeeze | solution.py:391
  3.7 0.8 %copy.18 = s32[1,1,8,2]{3,2,1,0:T(8,128)S(1)} copy(s32[1,1,8,2]{2,3,1,0:T(2,128)} %param.15) | data formatting | bytes 128 | tf_op args[7]
  4.4 0.1 reshape.30
  4.5 0.0 copy-start
  4.5 2.2 %copy-done = bf16[1,1,128,128,128]{4,3,2,1,0:T(8,128)(2,1)S(1)} copy-done((bf16[1,1,128,128,128]{4,3,2,1,0:T(8,128)(2,1)S(1)}, bf16[1,1,128,128,128]{4,3,2,1,0:T(8,128)(2,1)}, u32[]{:S(2)}) %copy-start) | copy-done | bytes 4194328
  6.7 0.0 copy-start.1
  6.7 0.9 %copy-done.1 = bf16[1,1,512,128]{3,2,1,0:T(8,128)(2,1)S(1)} copy-done((bf16[1,1,512,128]{3,2,1,0:T(8,128)(2,1)S(1)}, bf16[1,1,512,128]{3,2,1,0:T(8,128)(2,1)}, u32[]{:S(2)}) %copy-start.1) | copy-done | bytes 131096
  7.6 0.0 copy-start.2
  7.6 0.9 %copy-done.2 = bf16[1,1,512,128]{3,2,1,0:T(8,128)(2,1)S(1)} copy-done((bf16[1,1,512,128]{3,2,1,0:T(8,128)(2,1)S(1)}, bf16[1,1,512,128]{3,2,1,0:T(8,128)(2,1)}, u32[]{:S(2)}) %copy-start.2) | copy-done | bytes 131096
  8.5 0.0 copy-start.3
  8.5 0.8 %copy-done.3 = bf16[128,128]{1,0:T(8,128)(2,1)S(1)} copy-done((bf16[128,128]{1,0:T(8,128)(2,1)S(1)}, bf16[128,128]{1,0:T(8,128)(2,1)}, u32[]{:S(2)}) %copy-start.3) | copy-done | bytes 32792
  9.3 41.8 %shard_map.103 = (bf16[512,128]{1,0:T(8,128)(2,1)S(1)}, f32[128,128]{1,0:T(8,128)S(1)}, bf16[512,128]{1,0:T(8,128)(2,1)S(1)}) custom-call(s32[128]{0:T(128)S(1)} %select_reduce_fusion.inv, s32[8,2]{1,0:T(8,128)S(1)} %copy.19.col_need, s32[1,128]{1,0:T(1,128)S(1)} %pad.8.row_meta, s32[1,128]{1,0:T(1,128)S(1)} %pad.9.col_meta, ...), custom_call_target="tpu_custom_call" | custom-call | flops 1073741824 | bytes 4194304 | tf_op jit(solution)/shard_map/pallas_call | solution.py:333
  51.1 0.7 %copy.24 = bf16[1,1,512,128]{3,2,1,0:T(8,128)(2,1)} copy(bf16[1,1,512,128]{3,2,1,0:T(8,128)(2,1)S(1)} %bitcast.15) | data formatting | bytes 262144
  51.8 0.6 %copy.25 = f32[128,128]{1,0:T(8,128)} copy(f32[128,128]{1,0:T(8,128)S(1)} %get-tuple-element.13) | data formatting | bytes 131072
  52.4 0.7 %copy.26 = bf16[1,1,512,128]{3,2,1,0:T(8,128)(2,1)} copy(bf16[1,1,512,128]{3,2,1,0:T(8,128)(2,1)S(1)} %bitcast.14) | data formatting | bytes 262144
  (3 shorter events, 0.0 us)
Async XLA Ops:
  4.5 2.2 %copy-start = (bf16[1,1,128,128,128]{4,3,2,1,0:T(8,128)(2,1)S(1)}, bf16[1,1,128,128,128]{4,3,2,1,0:T(8,128)(2,1)}, u32[]{:S(2)}) copy-start(bf16[1,1,128,128,128]{4,3,2,1,0:T(8,128)(2,1)} %param.11) | copy-start | bytes 12582916
  6.7 0.9 %copy-start.1 = (bf16[1,1,512,128]{3,2,1,0:T(8,128)(2,1)S(1)}, bf16[1,1,512,128]{3,2,1,0:T(8,128)(2,1)}, u32[]{:S(2)}) copy-start(bf16[1,1,512,128]{3,2,1,0:T(8,128)(2,1)} %param.8) | copy-start | bytes 393220
  7.6 0.9 %copy-start.2 = (bf16[1,1,512,128]{3,2,1,0:T(8,128)(2,1)S(1)}, bf16[1,1,512,128]{3,2,1,0:T(8,128)(2,1)}, u32[]{:S(2)}) copy-start(bf16[1,1,512,128]{3,2,1,0:T(8,128)(2,1)} %param.9) | copy-start | bytes 393220
  8.5 0.8 %copy-start.3 = (bf16[128,128]{1,0:T(8,128)(2,1)S(1)}, bf16[128,128]{1,0:T(8,128)(2,1)}, u32[]{:S(2)}) copy-start(bf16[128,128]{1,0:T(8,128)(2,1)} %weight.1) | copy-start | bytes 98308

commit v2 on v1

v2 whole, which is shorter than its diff:
```python
import functools

import jax
import jax.numpy as jnp
from jax import lax
from jax.experimental import pallas as pl
from jax.experimental.pallas import tpu as pltpu
from jax.sharding import PartitionSpec as P

MESH = pl.DeviceIdType.MESH


def kernel(n_rows, n_cols, cap, scale, *refs):
    (
        live,
        col_own,
        slot,
        row_need,
        col_need,
        features,
        out_grad,
        weight,
        values,
        activated,
        weight_grad,
        input_grad,
    ) = refs[:12]
    (
        vals,
        w_vm,
        up_vm,
        slot_vm,
        inv_vm,
        inv_sm,
        acc,
        part_out,
        part_in,
        agg,
        back,
        back_out,
        back_in,
        dx_acc,
        dx_out,
        dx_in,
        row_vm,
        col_vm,
        row_sm,
        col_sm,
        wg_out,
        wg_in,
        wg_piece,
        wg_part,
        wg_sum,
        wg_done,
        local_sem,
        row_meta_s,
        row_meta_r,
        col_meta_s,
        col_meta_r,
        feat_s,
        feat_r,
        relay_s,
        relay_r,
        part_s,
        part_r,
        back_s,
        back_r,
        dx_s,
        dx_r,
        wg1_s,
        wg1_r,
        wg2_s,
        wg2_r,
        wg3_s,
        wg3_r,
    ) = refs[12:59]
    boxes = refs[59:]
    half = n_rows // 2
    direct, relayed = boxes[:half], boxes[half:]
    r_me, c_me = lax.axis_index("gr"), lax.axis_index("gc")
    r_other = r_me + 1 - 2 * lax.rem(r_me, 2)
    nzb, blk, _ = values.shape
    per_dev, _, width = features.shape
    col_slots, row_slots = n_rows * cap, n_cols * cap
    lanes = inv_vm.shape[1]

    def row_at(d):
        return lax.rem(r_me + d, n_rows)

    def col_at(d):
        return lax.rem(c_me + d, n_cols)

    def remote(axis, to, src, dst, send, recv):
        return pltpu.make_async_remote_copy(
            src_ref=src,
            dst_ref=dst,
            send_sem=send,
            recv_sem=recv,
            device_id={axis: to},
            device_id_type=MESH,
        )

    def to_row(d, src, dst, send, recv):
        return remote("gr", row_at(d), src, dst, send.at[d], recv.at[d])

    def to_col(d, src, dst, send, recv):
        return remote("gc", col_at(d), src, dst, send.at[d], recv.at[d])

    def each(n, body, start=1):
        def step(d, carry):
            body(d)
            return carry

        lax.fori_loop(start, n, step, 0)

    def inv_at(t, s):
        p = t * col_slots + s
        return inv_sm[lax.div(p, lanes), lax.rem(p, lanes)]

    loads = [
        pltpu.make_async_copy(src, dst, local_sem.at[n])
        for n, (src, dst) in enumerate(
            (
                (slot, slot_vm),
                (features, direct[0]),
                (values, vals.at[pl.ds(0, nzb)]),
                (row_need, row_vm.at[c_me]),
                (col_need, col_vm.at[r_me]),
                (weight, w_vm),
                (out_grad, up_vm),
            )
        )
    ]
    for load in loads:
        load.start()

    barrier = pltpu.get_barrier_semaphore()

    def greet_row(d):
        pl.semaphore_signal(barrier, inc=1, device_id={"gr": row_at(d)}, device_id_type=MESH)

    def greet_col(d):
        pl.semaphore_signal(barrier, inc=1, device_id={"gc": col_at(d)}, device_id_type=MESH)

    each(n_rows, greet_row)
    each(n_cols, greet_col)

    vals[nzb] = jnp.zeros((blk, blk), jnp.bfloat16)
    part_in[row_slots] = jnp.zeros((blk, width), jnp.bfloat16)
    dx_in[col_slots] = jnp.zeros((blk, width), jnp.bfloat16)
    pl.semaphore_wait(barrier, n_rows + n_cols - 2)

    def feat_copy(j):
        return remote(
            "gr", row_at(2 * j), features, direct[j], feat_s.at[j], feat_r.at[j]
        )

    def relay_copy(j):
        src = features if j == 0 else direct[j]
        return remote("gr", r_other, src, relayed[j], relay_s.at[j], relay_r.at[j])

    def row_meta_copy(d):
        return to_col(d, row_need, row_vm.at[c_me], row_meta_s, row_meta_r)

    def col_meta_copy(d):
        return to_row(d, col_need, col_vm.at[r_me], col_meta_s, col_meta_r)

    for j in range(1, half):
        feat_copy(j).start()
    relay_copy(0).start()
    each(n_cols, lambda d: row_meta_copy(d).start())
    each(n_rows, lambda d: col_meta_copy(d).start())

    loads[0].wait()
    turned_slot = jnp.broadcast_to(slot_vm[...], (lanes, nzb)).T
    block = lax.broadcasted_iota(jnp.int32, (nzb, lanes), 0)
    place = lax.broadcasted_iota(jnp.int32, (nzb, lanes), 1)
    alive = block < live[0, 0]
    for q in range(inv_vm.shape[0]):
        match = alive & (turned_slot == place + q * lanes)
        inv_vm[q : q + 1, :] = jnp.min(jnp.where(match, block, nzb), axis=0, keepdims=True)
    inv_load = pltpu.make_async_copy(inv_vm, inv_sm, local_sem.at[7])
    inv_load.start()
    inv_load.wait()
    loads[1].wait()
    loads[2].wait()

    group = min(row_slots, 8)

    def forward(box, owner, first=False):
        right = jnp.concatenate([box[col_own[c, owner]] for c in range(cap)], axis=0)

        def step(g):
            for q in range(group):
                t = g * group + q
                left = jnp.concatenate(
                    [vals[inv_at(t, owner * cap + c)] for c in range(cap)], axis=1
                )
                term = jnp.dot(left, right, preferred_element_type=jnp.float32)
                acc[t] = term if first else acc[t] + term

        if group == row_slots:
            step(0)
        else:
            each(row_slots // group, step, 0)

    forward(direct[0], r_me, True)
    relay_copy(0).wait()
    forward(relayed[0], r_other)
    for j in range(1, half):
        feat_copy(j).wait()
        relay_copy(j).start()
        forward(direct[j], lax.rem(r_me - 2 * j + n_rows, n_rows))
        if j > 1:
            relay_copy(j - 1).wait()
            forward(relayed[j - 1], lax.rem(r_other - 2 * (j - 1) + n_rows, n_rows))
    if half > 1:
        relay_copy(half - 1).wait()
        forward(relayed[half - 1], lax.rem(r_other - 2 * (half - 1) + n_rows, n_rows))

    def part_copy(d):
        src = part_out.at[pl.ds(col_at(d) * cap, cap)]
        return to_col(d, src, part_in.at[pl.ds(c_me * cap, cap)], part_s, part_r)

    def part_to(d):
        for k in range(cap):
            t = col_at(d) * cap + k
            part_out[t] = acc[t].astype(jnp.bfloat16)
        part_copy(d).start()

    each(n_cols, part_to)
    for k in range(cap):
        part_in[c_me * cap + k] = acc[c_me * cap + k].astype(jnp.bfloat16)

    loads[3].wait()
    loads[4].wait()
    each(n_cols, lambda d: row_meta_copy(d).wait())
    each(n_rows, lambda d: col_meta_copy(d).wait())
    row_load = pltpu.make_async_copy(row_vm, row_sm, local_sem.at[8])
    col_load = pltpu.make_async_copy(col_vm, col_sm, local_sem.at[9])
    row_load.start()
    col_load.start()
    loads[5].wait()
    loads[6].wait()
    row_load.wait()
    col_load.wait()
    each(n_cols, lambda d: part_copy(d).wait())

    def total_of(ref, asked, n, k):
        total = jnp.zeros((blk, width), jnp.float32)
        for o in range(n):
            at = n * cap
            for q in range(cap):
                at = jnp.where(asked[o][q] == k, o * cap + q, at)
            total = total + ref[at].astype(jnp.float32)
        return total.astype(jnp.bfloat16)

    row_asked = [[row_sm[o, q, c_me] for q in range(cap)] for o in range(n_cols)]
    for k in range(per_dev):
        agg[pl.ds(k * blk, blk), :] = total_of(part_in, row_asked, n_cols, k)
    held = agg[...]
    pre = jnp.dot(held, w_vm[...], preferred_element_type=jnp.float32)
    sig = jax.nn.sigmoid(pre)
    upstream = up_vm[...].astype(jnp.float32)
    grad_pre = (upstream * sig * (1.0 + pre * (1.0 - sig))).astype(jnp.bfloat16)
    rows = lax.dot_general(
        grad_pre, w_vm[...], (((1,), (1,)), ((), ())), preferred_element_type=jnp.float32
    ).astype(jnp.bfloat16)
    for k in range(per_dev):
        back[k] = rows[k * blk : (k + 1) * blk]

    def back_copy(d):
        src = back_out.at[pl.ds(col_at(d) * cap, cap)]
        return to_col(d, src, back_in.at[pl.ds(c_me * cap, cap)], back_s, back_r)

    def back_to(d):
        c = col_at(d)
        for k in range(cap):
            back_out[c * cap + k] = back[row_sm[c, k, c_me]]
        back_copy(d).start()

    each(n_cols, back_to)
    for k in range(cap):
        back_in[c_me * cap + k] = back[row_sm[c_me, k, c_me]]
    activated[...] = (pre * sig).astype(jnp.bfloat16)

    term = lax.dot_general(
        held, grad_pre, (((0,), (0,)), ((), ())), preferred_element_type=jnp.float32
    )
    piece = term.shape[0] // n_rows
    for o in range(n_rows):
        wg_out[o] = term[o * piece : (o + 1) * piece]
    wg_in[r_me] = wg_out[r_me]

    def wg1_copy(d):
        return to_row(d, wg_out.at[row_at(d)], wg_in.at[r_me], wg1_s, wg1_r)

    def wg2_copy(d):
        return to_col(d, wg_piece, wg_part.at[c_me], wg2_s, wg2_r)

    def wg3_copy(d):
        return to_row(d, wg_sum, wg_done.at[r_me], wg3_s, wg3_r)

    each(n_rows, lambda d: wg1_copy(d).start())

    def backward(turned, c, r):
        right = jnp.concatenate(
            [
                jnp.concatenate(
                    [vals[inv_at(c * cap + q, r * cap + k)] for k in range(cap)], axis=1
                )
                for q in range(cap)
            ],
            axis=0,
        )
        return jnp.dot(turned, right, preferred_element_type=jnp.float32)

    def turn(c):
        return back_in[pl.ds(c * cap, cap)].reshape(cap * blk, width).T

    group_r = min(n_rows, 8)

    def backward_all(c, first=False):
        turned = turn(c)

        def step(g):
            for q in range(group_r):
                r = g * group_r + q
                total = backward(turned, c, r)
                dx_acc[r] = total if first else dx_acc[r] + total

        if group_r == n_rows:
            step(0)
        else:
            each(n_rows // group_r, step, 0)

    backward_all(c_me, True)

    each(n_rows, lambda d: wg1_copy(d).wait())
    total = wg_in[0]
    for o in range(1, n_rows):
        total = total + wg_in[o]
    wg_piece[...] = total
    wg_part[c_me] = total
    each(n_cols, lambda d: wg2_copy(d).start())

    def source(d):
        return lax.rem(c_me - d + n_cols, n_cols)

    def backward_from(d):
        back_copy(d).wait()
        backward_all(source(d))

    each(n_cols - 1, backward_from)
    back_copy(n_cols - 1).wait()
    last = source(n_cols - 1)
    turned = turn(last)

    def dx_copy(d):
        src = dx_out.at[pl.ds(row_at(d) * cap, cap)]
        return to_row(d, src, dx_in.at[pl.ds(r_me * cap, cap)], dx_s, dx_r)

    def backward_last(r, ref):
        total = dx_acc[r] + backward(turned, last, r)
        for k in range(cap):
            ref[r * cap + k] = total[:, k * blk : (k + 1) * blk].T.astype(jnp.bfloat16)

    def backward_to(d):
        backward_last(row_at(d), dx_out)
        dx_copy(d).start()

    each(n_rows, backward_to)
    backward_last(r_me, dx_in)

    each(n_cols, lambda d: wg2_copy(d).wait())
    total = wg_part[0]
    for o in range(1, n_cols):
        total = total + wg_part[o]
    total = total * scale
    wg_sum[...] = total
    wg_done[r_me] = total
    each(n_rows, lambda d: wg3_copy(d).start())

    each(n_rows, lambda d: dx_copy(d).wait())
    col_asked = [[col_sm[o, q, r_me] for q in range(cap)] for o in range(n_rows)]
    for k in range(per_dev):
        input_grad[pl.ds(k * blk, blk), :] = total_of(dx_in, col_asked, n_rows, k)
    each(n_rows, lambda d: wg3_copy(d).wait())
    for o in range(n_rows):
        weight_grad[pl.ds(o * piece, piece), :] = wg_done[o]


def on_device(features, out_grad, weight, block_values, block_slot, live_count, row_need, col_need):
    n_rows = lax.axis_size("gr")
    n_cols = lax.axis_size("gc")
    values = block_values[0, 0]
    nzb, blk, _ = values.shape
    local, width = features.shape[2:]
    per_dev = local // blk
    cap = row_need.shape[3]
    col_slots = n_rows * cap
    row_slots = n_cols * cap
    bf, f32, i32 = jnp.bfloat16, jnp.float32, jnp.int32
    piece = width // n_rows
    places = col_slots * row_slots
    half = n_rows // 2
    dma = pltpu.SemaphoreType.DMA
    vmem = pl.BlockSpec(memory_space=pltpu.VMEM)
    smem = pl.BlockSpec(memory_space=pltpu.SMEM)
    hbm = pl.BlockSpec(memory_space=pltpu.HBM)
    scale = float(local * n_rows * n_cols) ** (-0.5)
    flops = 4 * nzb * blk * blk * width
    box = pltpu.VMEM((per_dev, blk, width), bf)
    rows_dma, cols_dma, half_dma = dma((n_rows,)), dma((n_cols,)), dma((half,))
    activated, weight_grad, input_grad = pl.pallas_call(
        functools.partial(kernel, n_rows, n_cols, cap, scale),
        out_shape=(
            jax.ShapeDtypeStruct((local, width), bf),
            jax.ShapeDtypeStruct((width, width), f32),
            jax.ShapeDtypeStruct((local, width), bf),
        ),
        in_specs=[smem, smem] + [hbm] * 7,
        out_specs=(vmem, vmem, vmem),
        scratch_shapes=[
            pltpu.VMEM((nzb + 1, blk, blk), bf),
            pltpu.VMEM((width, width), bf),
            pltpu.VMEM((local, width), bf),
            pltpu.VMEM((1, nzb), i32),
            pltpu.VMEM((places // 128, 128), i32),
            pltpu.SMEM((places // 128, 128), i32),
            pltpu.VMEM((row_slots, blk, width), f32),
            pltpu.VMEM((row_slots, blk, width), bf),
            pltpu.VMEM((row_slots + 1, blk, width), bf),
            pltpu.VMEM((local, width), bf),
            pltpu.VMEM((per_dev, blk, width), bf),
            pltpu.VMEM((row_slots, blk, width), bf),
            pltpu.VMEM((row_slots, blk, width), bf),
            pltpu.VMEM((n_rows, width, cap * blk), f32),
            pltpu.VMEM((col_slots, blk, width), bf),
            pltpu.VMEM((col_slots + 1, blk, width), bf),
            pltpu.VMEM((n_cols, cap, n_cols), i32),
            pltpu.VMEM((n_rows, cap, n_rows), i32),
            pltpu.SMEM((n_cols, cap, n_cols), i32),
            pltpu.SMEM((n_rows, cap, n_rows), i32),
            pltpu.VMEM((n_rows, piece, width), f32),
            pltpu.VMEM((n_rows, piece, width), f32),
            pltpu.VMEM((piece, width), f32),
            pltpu.VMEM((n_cols, piece, width), f32),
            pltpu.VMEM((piece, width), f32),
            pltpu.VMEM((n_rows, piece, width), f32),
            dma((10,)),
            cols_dma,
            cols_dma,
            rows_dma,
            rows_dma,
            half_dma,
            half_dma,
            half_dma,
            half_dma,
            cols_dma,
            cols_dma,
            cols_dma,
            cols_dma,
            rows_dma,
            rows_dma,
            rows_dma,
            rows_dma,
            cols_dma,
            cols_dma,
            rows_dma,
            rows_dma,
        ]
        + [box] * (2 * half),
        compiler_params=pltpu.CompilerParams(
            collective_id=0, has_side_effects=True, vmem_limit_bytes=48 * 2**20
        ),
        cost_estimate=pl.CostEstimate(
            flops=flops, bytes_accessed=values.size * 2, transcendentals=0
        ),
    )(
        live_count,
        col_need[0, 0].T,
        block_slot.reshape(1, nzb),
        row_need[0, 0].T,
        col_need[0, 0].T,
        features.reshape(per_dev, blk, width),
        out_grad.reshape(local, width),
        weight,
        values,
    )
    shape = (1, 1, local, width)
    return activated.reshape(shape), weight_grad, input_grad.reshape(shape)


def solution(mesh):
    placed = (
        P("gc", "gr", None, None),
        P("gr", "gc", None, None),
        P(),
        P("gr", "gc", None, None, None),
        P("gr", "gc", None),
        P("gr", "gc"),
        P("gr", "gc", None, None),
        P("gr", "gc", None, None),
    )
    return jax.shard_map(
        on_device,
        mesh=mesh,
        in_specs=placed,
        out_specs=(P("gr", "gc", None, None), P(), P("gc", "gr", None, None)),
        check_vma=False,
    )
```

time: 54.1 us -> 49.6 us (0.917); the launches traced: 53.1 us -> 49.3 us
  Pallas kernels: 41.8 us -> 39.3 us
  other arithmetic: 0.77 us -> 0 us
    pallas_call x1, Pallas kernels: 41.8 us -> 39.3 us  [on_device(): pl.pallas_call(functools.partial(kernel, n_rows, n_cols, cap, scale), out...]
    reduce_min x1 -> x0, other arithmetic: 0.77 us -> none  [on_device(): jnp.min(jnp.where(match, block[None, :], nzb), axis=1).astype(jnp.int32)]
    squeeze x1 -> x0, local copies, waits for them, and re-layouts: 0.75 us -> none  [on_device(): col_need[0, 0]]
    unnamed x13 -> x17, local copies, waits for them, and re-layouts: 8.21 us -> 8.7 us
where the time goes in v2:
time: 49.6 us; the launch traced here: 49.3 us
  Pallas kernels  39.3 us (79%)
  local copies, waits for them, and re-layouts  8.7 us (18%)
  between operations  1.3 us (3%)
    pallas_call x1, Pallas kernels, on_device(): pl.pallas_call(functools.partial(kernel, n_rows, n_cols, cap, scale), out...  39.3 us
    unnamed x17, local copies, waits for them, and re-layouts  8.7 us

profile of v2, /device:TPU:25, one launch (start us, length us, event | category | flops | bytes accessed | tf_op | source)
XLA Modules:
  0.0 49.3 jit_solution(17765328181077593464)
XLA Ops:
  1.3 0.0 copy-start
  1.3 2.2 %copy-done = bf16[1,1,128,128,128]{4,3,2,1,0:T(8,128)(2,1)S(1)} copy-done((bf16[1,1,128,128,128]{4,3,2,1,0:T(8,128)(2,1)S(1)}, bf16[1,1,128,128,128]{4,3,2,1,0:T(8,128)(2,1)}, u32[]{:S(2)}) %copy-start) | copy-done | bytes 4194328
  3.5 0.0 copy-start.1
  3.5 0.9 %copy-done.1 = bf16[1,1,512,128]{3,2,1,0:T(8,128)(2,1)S(1)} copy-done((bf16[1,1,512,128]{3,2,1,0:T(8,128)(2,1)S(1)}, bf16[1,1,512,128]{3,2,1,0:T(8,128)(2,1)}, u32[]{:S(2)}) %copy-start.1) | copy-done | bytes 131096
  4.4 0.0 copy-start.2
  4.4 0.9 %copy-done.2 = bf16[1,1,512,128]{3,2,1,0:T(8,128)(2,1)S(1)} copy-done((bf16[1,1,512,128]{3,2,1,0:T(8,128)(2,1)S(1)}, bf16[1,1,512,128]{3,2,1,0:T(8,128)(2,1)}, u32[]{:S(2)}) %copy-start.2) | copy-done | bytes 131096
  5.3 0.0 copy-start.3
  5.3 0.8 %copy-done.3 = bf16[128,128]{1,0:T(8,128)(2,1)S(1)} copy-done((bf16[128,128]{1,0:T(8,128)(2,1)S(1)}, bf16[128,128]{1,0:T(8,128)(2,1)}, u32[]{:S(2)}) %copy-start.3) | copy-done | bytes 32792
  6.0 0.0 copy-start.4
  6.0 0.7 %copy-done.4 = s32[1,1,8,2]{2,3,1,0:T(2,128)S(1)} copy-done((s32[1,1,8,2]{2,3,1,0:T(2,128)S(1)}, s32[1,1,8,2]{2,3,1,0:T(2,128)}, u32[]{:S(2)}) %copy-start.4) | copy-done | bytes 88
  6.7 0.0 copy-start.5
  6.7 0.7 %copy-done.5 = s32[1,1,4,2]{2,3,1,0:T(2,128)S(1)} copy-done((s32[1,1,4,2]{2,3,1,0:T(2,128)S(1)}, s32[1,1,4,2]{2,3,1,0:T(2,128)}, u32[]{:S(2)}) %copy-start.5) | copy-done | bytes 56
  7.4 0.0 copy-start.6
  7.4 0.7 %copy-done.6 = s32[1,1,128]{2,1,0:T(1,128)S(1)} copy-done((s32[1,1,128]{2,1,0:T(1,128)S(1)}, s32[1,1,128]{2,1,0:T(1,128)}, u32[]{:S(2)}) %copy-start.6) | copy-done | bytes 536
  8.1 39.3 %shard_map.103 = (bf16[512,128]{1,0:T(8,128)(2,1)S(1)}, f32[128,128]{1,0:T(8,128)S(1)}, bf16[512,128]{1,0:T(8,128)(2,1)S(1)}) custom-call(s32[1,1]{1,0:T(1,128)S(6)} %copy.14.refs_0_, s32[2,8]{1,0:T(2,128)S(1)} %bitcast.17, s32[1,128]{1,0:T(1,128)S(1)} %bitcast.20, s32[2,4]{1,0:T(2,128)S(1)} %bitcast.19, s32[2,8]{1,0:T(2,128)S(1)} %bitcast.18, ...), custom_call_target="tpu_custom_call" | custom-call | flops 1073741824 | bytes 4194304 | tf_op jit(solution)/shard_map/pallas_call | solution.py:415
  47.4 0.7 %copy.15 = bf16[1,1,512,128]{3,2,1,0:T(8,128)(2,1)} copy(bf16[1,1,512,128]{3,2,1,0:T(8,128)(2,1)S(1)} %bitcast.16) | data formatting | bytes 262144
  48.0 0.6 %copy.16 = f32[128,128]{1,0:T(8,128)} copy(f32[128,128]{1,0:T(8,128)S(1)} %get-tuple-element.13) | data formatting | bytes 131072
  48.6 0.7 %copy.17 = bf16[1,1,512,128]{3,2,1,0:T(8,128)(2,1)} copy(bf16[1,1,512,128]{3,2,1,0:T(8,128)(2,1)S(1)} %bitcast.15) | data formatting | bytes 262144
Async XLA Ops:
  1.3 2.2 %copy-start = (bf16[1,1,128,128,128]{4,3,2,1,0:T(8,128)(2,1)S(1)}, bf16[1,1,128,128,128]{4,3,2,1,0:T(8,128)(2,1)}, u32[]{:S(2)}) copy-start(bf16[1,1,128,128,128]{4,3,2,1,0:T(8,128)(2,1)} %param.11) | copy-start | bytes 12582916
  3.5 0.9 %copy-start.1 = (bf16[1,1,512,128]{3,2,1,0:T(8,128)(2,1)S(1)}, bf16[1,1,512,128]{3,2,1,0:T(8,128)(2,1)}, u32[]{:S(2)}) copy-start(bf16[1,1,512,128]{3,2,1,0:T(8,128)(2,1)} %param.8) | copy-start | bytes 393220
  4.4 0.9 %copy-start.2 = (bf16[1,1,512,128]{3,2,1,0:T(8,128)(2,1)S(1)}, bf16[1,1,512,128]{3,2,1,0:T(8,128)(2,1)}, u32[]{:S(2)}) copy-start(bf16[1,1,512,128]{3,2,1,0:T(8,128)(2,1)} %param.9) | copy-start | bytes 393220
  5.3 0.8 %copy-start.3 = (bf16[128,128]{1,0:T(8,128)(2,1)S(1)}, bf16[128,128]{1,0:T(8,128)(2,1)}, u32[]{:S(2)}) copy-start(bf16[128,128]{1,0:T(8,128)(2,1)} %refs_7_.1) | copy-start | bytes 98308
  6.0 0.7 %copy-start.4 = (s32[1,1,8,2]{2,3,1,0:T(2,128)S(1)}, s32[1,1,8,2]{2,3,1,0:T(2,128)}, u32[]{:S(2)}) copy-start(s32[1,1,8,2]{2,3,1,0:T(2,128)} %param.15) | copy-start | bytes 196
  6.7 0.7 %copy-start.5 = (s32[1,1,4,2]{2,3,1,0:T(2,128)S(1)}, s32[1,1,4,2]{2,3,1,0:T(2,128)}, u32[]{:S(2)}) copy-start(s32[1,1,4,2]{2,3,1,0:T(2,128)} %param.14) | copy-start | bytes 100
  7.4 0.7 %copy-start.6 = (s32[1,1,128]{2,1,0:T(1,128)S(1)}, s32[1,1,128]{2,1,0:T(1,128)}, u32[]{:S(2)}) copy-start(s32[1,1,128]{2,1,0:T(1,128)} %param.12) | copy-start | bytes 1540

commit v3 on v2

--- a/solution.py
+++ b/solution.py
@@ -148,28 +148,6 @@
     vals[nzb] = jnp.zeros((blk, blk), jnp.bfloat16)
     part_in[row_slots] = jnp.zeros((blk, width), jnp.bfloat16)
     dx_in[col_slots] = jnp.zeros((blk, width), jnp.bfloat16)
-    pl.semaphore_wait(barrier, n_rows + n_cols - 2)
-
-    def feat_copy(j):
-        return remote(
-            "gr", row_at(2 * j), features, direct[j], feat_s.at[j], feat_r.at[j]
-        )
-
-    def relay_copy(j):
-        src = features if j == 0 else direct[j]
-        return remote("gr", r_other, src, relayed[j], relay_s.at[j], relay_r.at[j])
-
-    def row_meta_copy(d):
-        return to_col(d, row_need, row_vm.at[c_me], row_meta_s, row_meta_r)
-
-    def col_meta_copy(d):
-        return to_row(d, col_need, col_vm.at[r_me], col_meta_s, col_meta_r)
-
-    for j in range(1, half):
-        feat_copy(j).start()
-    relay_copy(0).start()
-    each(n_cols, lambda d: row_meta_copy(d).start())
-    each(n_rows, lambda d: col_meta_copy(d).start())
 
     loads[0].wait()
     turned_slot = jnp.broadcast_to(slot_vm[...], (lanes, nzb)).T
@@ -205,6 +183,29 @@
             each(row_slots // group, step, 0)
 
     forward(direct[0], r_me, True)
+
+    def feat_copy(j):
+        return remote(
+            "gr", row_at(2 * j), features, direct[j], feat_s.at[j], feat_r.at[j]
+        )
+
+    def relay_copy(j):
+        src = features if j == 0 else direct[j]
+        return remote("gr", r_other, src, relayed[j], relay_s.at[j], relay_r.at[j])
+
+    def row_meta_copy(d):
+        return to_col(d, row_need, row_vm.at[c_me], row_meta_s, row_meta_r)
+
+    def col_meta_copy(d):
+        return to_row(d, col_need, col_vm.at[r_me], col_meta_s, col_meta_r)
+
+    pl.semaphore_wait(barrier, n_rows + n_cols - 2)
+    for j in range(1, half):
+        feat_copy(j).start()
+    relay_copy(0).start()
+    each(n_cols, lambda d: row_meta_copy(d).start())
+    each(n_rows, lambda d: col_meta_copy(d).start())
+
     relay_copy(0).wait()
     forward(relayed[0], r_other)
     for j in range(1, half):
@@ -388,6 +389,19 @@
     each(n_rows, lambda d: wg3_copy(d).wait())
     for o in range(n_rows):
         weight_grad[pl.ds(o * piece, piece), :] = wg_done[o]
+
+
+def hand_over(n, *refs):
+    srcs, dsts, boxes, sem = refs[:n], refs[n : 2 * n], refs[2 * n : 3 * n], refs[3 * n]
+    inward = [pltpu.make_async_copy(srcs[k], boxes[k], sem.at[k]) for k in range(n)]
+    outward = [pltpu.make_async_copy(boxes[k], dsts[k], sem.at[n + k]) for k in range(n)]
+    for copy in inward:
+        copy.start()
+    for k in range(n):
+        inward[k].wait()
+        outward[k].start()
+    for copy in outward:
+        copy.wait()
 
 
 def on_device(features, out_grad, weight, block_values, block_slot, live_count, row_need, col_need):
@@ -472,7 +486,7 @@
         ]
         + [box] * (2 * half),
         compiler_params=pltpu.CompilerParams(
-            collective_id=0, has_side_effects=True, vmem_limit_bytes=48 * 2**20
+            collective_id=0, has_side_effects=True, vmem_limit_bytes=60 * 2**20
         ),
         cost_estimate=pl.CostEstimate(
             flops=flops, bytes_accessed=values.size * 2, transcendentals=0
@@ -488,6 +502,15 @@
         weight,
         values,
     )
+    anywhere = pl.BlockSpec(memory_space=pl.ANY)
+    outs = (activated, weight_grad, input_grad)
+    activated, weight_grad, input_grad = pl.pallas_call(
+        functools.partial(hand_over, len(outs)),
+        out_shape=[jax.ShapeDtypeStruct(o.shape, o.dtype) for o in outs],
+        in_specs=[anywhere] * 3,
+        out_specs=[anywhere] * 3,
+        scratch_shapes=[pltpu.VMEM(o.shape, o.dtype) for o in outs] + [dma((2 * len(outs),))],
+    )(*outs)
     shape = (1, 1, local, width)
     return activated.reshape(shape), weight_grad, input_grad.reshape(shape)
 

time: 49.6 us -> 43 us (0.87)
  local copies, waits for them, and re-layouts: 8.7 us -> 0 us
  Pallas kernels: 39.3 us -> 41.5 us
    unnamed x17 -> x0, local copies, waits for them, and re-layouts: 8.7 us -> none
    pallas_call x0 -> x1, Pallas kernels: none -> 1.71 us  [on_device(): pl.pallas_call(functools.partial(hand_over, len(outs)), out_shape=[jax.Sh...]
    pallas_call x1, Pallas kernels: 39.3 us -> 39.8 us  [on_device(): pl.pallas_call(functools.partial(kernel, n_rows, n_cols, cap, scale), out...]
where the time goes in v3:
time: 43 us; the launch traced here: 42.8 us
  Pallas kernels  41.5 us (97%)
  between operations  1.29 us (3%)
    pallas_call x1, Pallas kernels, on_device(): pl.pallas_call(functools.partial(kernel, n_rows, n_cols, cap, scale), out...  39.8 us
    pallas_call x1, Pallas kernels, on_device(): pl.pallas_call(functools.partial(hand_over, len(outs)), out_shape=[jax.Sh...  1.71 us

profile of v3, /device:TPU:25, one launch (start us, length us, event | category | flops | bytes accessed | tf_op | source)
XLA Modules:
  0.0 42.8 jit_solution(12323676149243023892)
XLA Ops:
  1.3 39.8 %shard_map.103 = (bf16[512,128]{1,0:T(8,128)(2,1)}, f32[128,128]{1,0:T(8,128)}, bf16[512,128]{1,0:T(8,128)(2,1)}) custom-call(s32[1,1]{1,0:T(1,128)S(6)} %copy.11.refs_0_, s32[2,8]{1,0:T(2,128)} %bitcast.15, s32[1,128]{1,0:T(1,128)} %bitcast.18, s32[2,4]{1,0:T(2,128)} %bitcast.17, s32[2,8]{1,0:T(2,128)} %bitcast.16, bf16[4,128,128]{2,1,0:T(8,128)(2,1)} %bitcast.13, ...), custom_call_target="tpu_custom_call" | custom-call | flops 1073741824 | bytes 4194304 | tf_op jit(solution)/shard_map/pallas_call | solution.py:429
  41.1 1.7 %shard_map.104 = (bf16[512,128]{1,0:T(8,128)(2,1)}, f32[128,128]{1,0:T(8,128)}, bf16[512,128]{1,0:T(8,128)(2,1)}) custom-call(bf16[512,128]{1,0:T(8,128)(2,1)} %get-tuple-element.9.refs_0_, f32[128,128]{1,0:T(8,128)} %get-tuple-element.10.refs_1_, bf16[512,128]{1,0:T(8,128)(2,1)} %get-tuple-element.11.refs_2_), custom_call_target="tpu_custom_call" | custom-call | tf_op jit(solution)/shard_map/pallas_call | solution.py:507
